TPU v7x, 32 devices: a whole 2x2x4 slice. The times are simulated.
32 devices in a mesh: groups: 2 (over x), dp: 16 (over z, y, core).
Axes of the slice: x: 2, y: 2, z: 4, core: 2. Of those that a mesh axis runs over, the one named last changes fastest.
Arguments:
- embeddings: bfloat16 [96, 512, 256], P(('groups', 'dp')), parts along dimension 0, may hold values from -6 to 6
- projection: bfloat16 [512, 64], replicated, may hold values from -0.25 to 0.25
- norm_gain: float32 [16384], replicated, may hold values from 0.5 to 1.5
- norm_bias: float32 [16384], replicated, may hold values from -3 to 3
- up_weight: bfloat16 [16384, 4096], P('dp'), may hold values from -0.046875 to 0.046875
- up_bias: float32 [4096], replicated, may hold values from -3 to 3
- down_weight: bfloat16 [4096, 16384], P(None, 'dp'), may hold values from -0.09375 to 0.09375
- cotangent: bfloat16 [96, 16384], P('groups', 'dp'), parts along dimension 0, may hold values from -0.59765625 to 0.59765625
Outputs:
- interaction_out: bfloat16 [96, 16384], P('groups', 'dp'), parts along dimension 0
- grad_embeddings: bfloat16 [96, 512, 256], P(('groups', 'dp')), parts along dimension 0
- grad_projection: float32 [1024, 64], P('groups'), parts along dimension 0
- grad_gain: float32 [32768], P('groups'), parts along dimension 0
- grad_bias: float32 [32768], P('groups'), parts along dimension 0
- grad_up: float32 [32768, 4096], P(('groups', 'dp')), parts along dimension 0
- grad_up_bias: float32 [8192], P('groups'), parts along dimension 0
- grad_down: float32 [8192, 16384], P('groups', 'dp'), parts along dimension 0
There are 2 independent parts, one for each index of `groups`. A program takes and returns all parts, laid end to end along the dimension named above; an argument that names none is the same for every part. Nothing has to cross between parts.
All inputs are finite; a program needn't handle non-finite values.
Results may differ from a plain program's by a relative error of at most 0.01.
Values may be sent and summed in bfloat16 or wider, within the bound.
A program may use at most 128 MiB of HBM per device.

v0:
```python
import jax
import jax.numpy as jnp
from jax import lax
from jax.sharding import PartitionSpec as P

epsilon = 1e-05


def activate(values):
    return jax.nn.gelu(values, approximate=True)


def activate_back(preact, grad_hidden):
    _, pullback = jax.vjp(activate, preact)
    return pullback(grad_hidden)[0]


def interact_row(sample, projection):
    pair_dots = jnp.dot(sample, sample.T, preferred_element_type=jnp.float32).astype(jnp.bfloat16)
    compressed = jnp.dot(pair_dots, projection, preferred_element_type=jnp.float32).astype(
        jnp.bfloat16
    )
    interaction = jnp.dot(sample.T, compressed, preferred_element_type=jnp.float32)
    return interaction.reshape(-1)


def interact_back(sample, projection, grad_flat):
    pair_dots = jnp.dot(sample, sample.T, preferred_element_type=jnp.float32).astype(jnp.bfloat16)
    compressed = jnp.dot(pair_dots, projection, preferred_element_type=jnp.float32).astype(
        jnp.bfloat16
    )
    grad_matrix = grad_flat.reshape(sample.shape[1], projection.shape[1])
    grad_compressed = jnp.dot(sample, grad_matrix, preferred_element_type=jnp.float32).astype(
        jnp.bfloat16
    )
    grad_direct = jnp.dot(compressed, grad_matrix.T, preferred_element_type=jnp.float32)
    grad_pairs = jnp.dot(grad_compressed, projection.T, preferred_element_type=jnp.float32).astype(
        jnp.bfloat16
    )
    grad_sample = grad_direct + jnp.dot(grad_pairs, sample, preferred_element_type=jnp.float32)
    grad_sample = grad_sample + jnp.dot(grad_pairs.T, sample, preferred_element_type=jnp.float32)
    grad_proj = jnp.dot(pair_dots.T, grad_compressed, preferred_element_type=jnp.float32)
    return (grad_sample.astype(jnp.bfloat16), grad_proj)


def layer_norm(interaction):
    centre = interaction - jnp.mean(interaction, axis=-1, keepdims=True)
    variance = jnp.mean(centre * centre, axis=-1, keepdims=True)
    inv_scale = lax.rsqrt(variance + epsilon)
    return (centre * inv_scale, inv_scale)


def norm_back(grad_normed, standard, inv_scale, norm_gain):
    scaled = grad_normed * norm_gain
    first = jnp.mean(scaled, axis=-1, keepdims=True)
    second = jnp.mean(scaled * standard, axis=-1, keepdims=True)
    return inv_scale * (scaled - first - standard * second)


def sum_rows(term, own_rows):
    return lax.psum_scatter(
        term(jnp.int32(0), lax.axis_size("dp") * own_rows), "dp", scatter_dimension=0, tiled=True
    )


def fold_rows(values, step_fn, initial):
    return step_fn(initial, lax.all_gather(values, "dp", axis=0, tiled=True), jnp.int32(0))


def contract_rows(left, right):
    return lax.dot_general(
        left, right, (((0,), (0,)), ((), ())), preferred_element_type=jnp.float32
    )


def contract_last(left, right):
    return lax.dot_general(
        left, right, (((1,), (1,)), ((), ())), preferred_element_type=jnp.float32
    )


def body(embeddings, projection, norm_gain, norm_bias, up_weight, up_bias, down_weight, cotangent):
    own_rows = embeddings.shape[0]
    interaction = jax.vmap(lambda sample: interact_row(sample, projection))(embeddings)
    standard, inv_scale = layer_norm(interaction)
    normed = (standard * norm_gain + norm_bias).astype(jnp.bfloat16)
    columns = lax.all_to_all(normed, "dp", split_axis=1, concat_axis=0, tiled=True)
    all_rows = columns.shape[0]
    own_features = up_weight.shape[0]
    hidden_units = up_weight.shape[1]

    def preact_term(offset, amount):
        return jnp.dot(columns, up_weight, preferred_element_type=jnp.float32)

    preact = sum_rows(preact_term, own_rows) + up_bias
    hidden = activate(preact).astype(jnp.bfloat16)

    def output_step(running, block_rows, offset):
        product = jnp.dot(block_rows, down_weight, preferred_element_type=jnp.float32)
        down_acc = contract_rows(block_rows, cotangent)
        return (product, down_acc)

    start_state = (
        jnp.zeros((all_rows, down_weight.shape[1]), jnp.float32),
        jnp.zeros(down_weight.shape, jnp.float32),
    )
    out_columns, grad_down = fold_rows(hidden, output_step, start_state)

    def hidden_term(offset, amount):
        return contract_last(cotangent, down_weight)

    grad_hidden = sum_rows(hidden_term, own_rows)
    grad_preact = activate_back(preact, grad_hidden).astype(jnp.bfloat16)

    def gradient_step(running, block_rows, offset):
        product = contract_last(block_rows, up_weight)
        up_acc = contract_rows(columns, block_rows)
        bias_acc = jnp.sum(block_rows.astype(jnp.float32), axis=0)
        return (product, up_acc, bias_acc)

    start_grad = (
        jnp.zeros((all_rows, own_features), jnp.float32),
        jnp.zeros(up_weight.shape, jnp.float32),
        jnp.zeros((hidden_units,), jnp.float32),
    )
    back_columns, grad_up, grad_up_bias = fold_rows(grad_preact, gradient_step, start_grad)
    grad_normed = lax.all_to_all(
        back_columns.astype(jnp.bfloat16), "dp", split_axis=0, concat_axis=1, tiled=True
    ).astype(jnp.float32)
    gain_part = jnp.sum(grad_normed * standard, axis=0)
    bias_part = jnp.sum(grad_normed, axis=0)
    grad_interaction = norm_back(grad_normed, standard, inv_scale, norm_gain).astype(jnp.bfloat16)
    grad_embeddings, proj_rows = jax.vmap(
        lambda sample, grad_flat: interact_back(sample, projection, grad_flat)
    )(embeddings, grad_interaction)
    proj_part = jnp.sum(proj_rows, axis=0)
    grad_projection, grad_gain, grad_bias = lax.psum((proj_part, gain_part, bias_part), "dp")
    return (
        out_columns.astype(jnp.bfloat16),
        grad_embeddings,
        grad_projection,
        grad_gain,
        grad_bias,
        grad_up,
        grad_up_bias,
        grad_down,
    )


def solution(mesh):
    return jax.shard_map(
        body,
        mesh=mesh,
        in_specs=(
            P(("groups", "dp"), None, None),
            P(),
            P(),
            P(),
            P("dp", None),
            P(),
            P(None, "dp"),
            P("groups", "dp"),
        ),
        out_specs=(
            P("groups", "dp"),
            P(("groups", "dp"), None, None),
            P("groups", None),
            P("groups"),
            P("groups"),
            P(("groups", "dp"), None),
            P("groups"),
            P("groups", "dp"),
        ),
        check_vma=False,
    )
```

profile of v0, /device:TPU:0, one launch (start us, length us, event | category | flops | bytes accessed | tf_op | source)
XLA Modules:
  0.0 325.3 jit_solution(109626224612486218)
XLA Ops:
  7.2 0.0 copy-start
  7.2 0.9 mul.120
  8.1 0.0 copy-start.3
  8.1 1.5 add.53
  9.6 0.0 copy-done
  9.6 0.6 convolution_convert_fusion.1
  10.3 0.2 copy-done.5
  10.5 0.6 convolution_convert_fusion.2
  11.1 0.0 copy-start.4
  11.1 0.4 fusion.13
  11.4 0.2 multiply_reduce_fusion.2
  11.7 0.2 copy.23
  11.8 0.2 reshape.139
  12.0 0.0 copy-done.3
  12.0 0.0 copy-start.1
  12.0 1.0 add_convert_fusion.1
  13.0 0.7 copy.24
  13.8 7.4 %all-to-all-start = ((bf16[3,16,1024]{2,0,1:T(4,128)(2,1)}), bf16[3,16,1024]{2,0,1:T(4,128)(2,1)S(1)}, u32[]{:S(2)}, u32[]{:S(2)}) async-start(bf16[3,16,1024]{2,0,1:T(4,128)(2,1)} %copy.24), calls=%async_computation | async-start | bytes 262144 | tf_op jit(solution)/shard_map/all_to_all | solution.py:87
  21.2 0.0 all-reduce.9.cloned.1.call-start
  21.2 0.0 copy-done.4
  21.2 6.9 %fusion.15 = f32[48,4096]{1,0:T(8,128)} fusion(bf16[48,1024]{1,0:T(8,128)(2,1)S(1)} %copy-done.4, bf16[4096,1024]{1,0:T(8,128)(2,1)} %param.14), kind=kOutput, calls=%fused_computation.40 | convolution fusion | flops 402653184 | bytes 9273344 | tf_op jit(solution)/shard_map/dot_general | solution.py:77
  28.1 0.0 copy-done.1
  28.1 1.0 all-to-all-done
  29.1 0.1 all_to_all.24
  29.2 5.8 %fusion.14 = f32[48,4096]{1,0:T(8,128)} fusion(bf16[48,1024]{1,0:T(8,128)(2,1)S(1)} %all_to_all.24, bf16[1024,4096]{1,0:T(8,128)(2,1)} %param.12), kind=kOutput, calls=%fused_computation.39 | convolution fusion | flops 402653184 | bytes 9273344 | tf_op jit(solution)/shard_map/dot_general | solution.py:93
  35.0 0.0 all-reduce.9.cloned.1.call-update
  35.1 0.8 copy-done.7
  35.9 0.1 mul.139
  35.9 0.7 copy.26
  36.7 0.6 dynamic-slice
  37.9 93.3 %all-reduce.9.cloned.1.call-done = (f32[48,4096]{1,0:T(8,128)}, f32[48,4096]{1,0:T(8,128)}) async-done(((f32[48,4096]{1,0:T(8,128)}, f32[48,4096]{1,0:T(8,128)}), (f32[48,4096]{1,0:T(8,128)}, f32[48,4096]{1,0:T(8,128)})) %all-reduce.9.cloned.1.call-update) | async-done | bytes 1572880
  131.2 1.2 fusion.12
  132.4 22.1 %all-gather.1 = bf16[16,3,4096]{2,1,0:T(4,128)(2,1)} all-gather(bf16[1,3,4096]{2,1,0:T(4,128)(2,1)S(1)} %get-tuple-element.17), channel_id=1, replica_groups=mesh['groups'=2,'dp'=16] {'dp'}, dimensions={0}, use_global_device_ids=true | all-gather | bytes 417792 | tf_op jit(solution)/shard_map/all_gather | solution.py:67
  154.5 1.4 reshape.144
  155.9 6.0 %convolution_convert_fusion.4 = bf16[48,1024]{1,0:T(8,128)(2,1)S(1)} fusion(bf16[48,4096]{1,0:T(8,128)(2,1)S(1)} %reshape.144, bf16[1024,4096]{1,0:T(8,128)(2,1)} %param.12), kind=kOutput, calls=%fused_computation.6 | convolution fusion | flops 402702336 | bytes 8880128 | tf_op jit(solution)/shard_map/dot_general | solution.py:77
  161.9 8.5 %fusion.18 = f32[1024,4096]{1,0:T(8,128)} fusion(bf16[48,1024]{1,0:T(8,128)(2,1)S(1)} %all_to_all.24, bf16[48,4096]{1,0:T(8,128)(2,1)S(1)} %reshape.144), kind=kOutput, calls=%fused_computation.43 | convolution fusion | flops 402653184 | bytes 17268736 | tf_op jit(solution)/shard_map/dot_general | solution.py:71
  170.4 0.7 all_to_all.25
  171.1 4.2 %all-to-all-start.1 = ((bf16[16,3,1024]{2,1,0:T(4,128)(2,1)}), bf16[16,3,1024]{2,1,0:T(4,128)(2,1)}, u32[]{:S(2)}, u32[]{:S(2)}) async-start(bf16[16,3,1024]{2,1,0:T(4,128)(2,1)} %all_to_all.25), calls=%async_computation.1 | async-start | bytes 262144 | tf_op jit(solution)/shard_map/all_to_all | solution.py:127
  175.3 0.0 all-reduce.7.cloned.1.call-start
  175.4 24.7 %all-gather = bf16[16,3,4096]{2,1,0:T(4,128)(2,1)} all-gather(bf16[1,3,4096]{2,1,0:T(4,128)(2,1)S(1)} %get-tuple-element.18), channel_id=1, replica_groups=mesh['groups'=2,'dp'=16] {'dp'}, dimensions={0}, use_global_device_ids=true | all-gather | bytes 417792 | tf_op jit(solution)/shard_map/all_gather | solution.py:67
  200.1 1.4 reshape.142
  201.4 9.4 %fusion.19 = f32[4096,1024]{1,0:T(8,128)} fusion(bf16[48,4096]{1,0:T(8,128)(2,1)S(1)} %reshape.142, bf16[48,1024]{1,0:T(8,128)(2,1)} %param.15), kind=kOutput, calls=%fused_computation.44 | convolution fusion | flops 402653184 | bytes 17268736 | tf_op jit(solution)/shard_map/dot_general | solution.py:71
  210.9 5.6 %convolution_convert_fusion.5 = bf16[48,1024]{1,0:T(8,128)(2,1)} fusion(bf16[48,4096]{1,0:T(8,128)(2,1)S(1)} %reshape.142, bf16[4096,1024]{1,0:T(8,128)(2,1)} %param.14), kind=kOutput, calls=%fused_computation.7 | convolution fusion | flops 402702336 | bytes 8880128 | tf_op jit(solution)/shard_map/dot_general | solution.py:99
  216.4 0.7 convert_reduce_fusion
  217.1 0.0 all-to-all-done.1
  217.1 0.9 convert_bitcast_fusion
  218.1 0.1 reshape.140
  218.2 0.1 copy.27
  218.4 1.1 multiply_reduce_fusion
  219.5 1.0 multiply_convert_fusion
  220.5 0.4 fusion
  220.8 0.0 copy-start.6
  220.8 1.6 fusion.16
  222.4 1.0 convolution_bitcast_fusion
  223.5 0.6 convolution_convert_fusion
  224.1 0.6 copy.30
  224.7 0.6 copy.31
  225.3 1.7 fusion.17
  227.1 0.0 all-reduce.7.cloned.1.call-update
  227.1 3.5 %add_convert_fusion = bf16[3,512,256]{2,1,0:T(8,128)(2,1)} fusion(f32[3,512,256]{2,1,0:T(8,128)} %fusion.16, f32[3,512,256]{2,1,0:T(8,128)} %fusion.17, bf16[3,512,512]{2,1,0:T(8,128)(2,1)S(1)} %convolution_convert_fusion, bf16[3,512,256]{2,1,0:T(8,128)(2,1)S(1)} %copy-done), kind=kOutput, calls=%fused_computation.2 | convolution fusion | flops 403832832 | bytes 6291456 | tf_op jit(solution)/shard_map/vmap()/dot_general | solution.py:41
  230.6 83.4 %all-reduce.7.cloned.1.call-done = (f32[512,64]{0,1:T(8,128)}, f32[16384]{0:T(1024)}, f32[16384]{0:T(1024)}) async-done(((f32[512,64]{0,1:T(8,128)}, f32[16384]{0:T(1024)}, f32[16384]{0:T(1024)}), (f32[512,64]{0,1:T(8,128)}, f32[16384]{0:T(1024)}, f32[16384]{0:T(1024)})) %all-reduce.7.cloned.1.call-update) | async-done | bytes 262160 | tf_op jit(solution)/shard_map/psum | solution.py:137
  313.9 1.6 copy.42
  315.5 1.5 copy.43
  317.0 1.5 copy.44
  (12 shorter events, 0.0 us)
Async XLA Ops:
  7.2 2.5 copy-start
  8.1 3.9 %copy-start.3 = (f32[16,1024]{1,0:T(8,128)}, f32[16,1024]{1,0:T(8,128)S(1)}, u32[]{:S(2)}) copy-start(f32[16,1024]{1,0:T(8,128)S(1)} %mul.120) | copy-start | bytes 196612
  9.6 0.8 copy-start.5
  11.1 10.1 %copy-start.4 = (bf16[48,1024]{1,0:T(8,128)(2,1)S(1)}, bf16[48,1024]{1,0:T(8,128)(2,1)}, u32[]{:S(2)}) copy-start(bf16[48,1024]{1,0:T(8,128)(2,1)} %param.15) | copy-start | bytes 294916
  12.0 16.1 %copy-start.1 = (f32[3,16,1024]{2,1,0:T(8,128)}, f32[3,16,1024]{2,1,0:T(8,128)S(1)}, u32[]{:S(2)}) copy-start(f32[3,16,1024]{2,1,0:T(8,128)S(1)} %reshape.139) | copy-start | bytes 589828
  13.8 15.3 %all-to-all-start = ((bf16[3,16,1024]{2,0,1:T(4,128)(2,1)}), bf16[3,16,1024]{2,0,1:T(4,128)(2,1)S(1)}, u32[]{:S(2)}, u32[]{:S(2)}) async-start(bf16[3,16,1024]{2,0,1:T(4,128)(2,1)} %copy.24), calls=%async_computation | async-start | bytes 262144 | tf_op jit(solution)/shard_map/all_to_all | solution.py:87
  21.2 110.1 %all-reduce.9.cloned.1.call-start = ((), (), s32[]{:S(2)}) async-start(), calls=%async_computation.3 | async-start | bytes 3145728
  35.0 0.8 copy-start.7
  35.0 1.6 copy-start.9
  35.0 96.2 %copy-start.8 = (f32[4096]{0:T(1024)S(1)}, f32[4096]{0:T(1024)}, u32[]{:S(2)}) copy-start(f32[4096]{0:T(1024)} %param.13) | copy-start | bytes 49156
  171.1 46.0 %all-to-all-start.1 = ((bf16[16,3,1024]{2,1,0:T(4,128)(2,1)}), bf16[16,3,1024]{2,1,0:T(4,128)(2,1)}, u32[]{:S(2)}, u32[]{:S(2)}) async-start(bf16[16,3,1024]{2,1,0:T(4,128)(2,1)} %all_to_all.25), calls=%async_computation.1 | async-start | bytes 262144 | tf_op jit(solution)/shard_map/all_to_all | solution.py:127
  175.3 138.6 %all-reduce.7.cloned.1.call-start = ((), (), s32[]{:S(2)}) async-start(), calls=%async_computation.2 | async-start | bytes 524288 | tf_op jit(solution)/shard_map/psum | solution.py:137
  216.4 1.9 copy-start.2
  220.8 2.6 copy-start.6
Sparse Core Ops, SparseCore 0:
  35.2 96.0 all-reduce.8
  227.2 86.6 all-reduce.6
where the time goes:
time: 326 us; the launch traced here: 325 us
  waiting for transfers between devices  178 us (55%)
  matrix products  52.6 us (16%)
  blocking collectives  46.8 us (14%)
  local copies, waits for them, and re-layouts  15.6 us (5%)
  between operations  14.9 us (5%)
  starting transfers between devices  11.6 us (4%)
  other arithmetic  6.1 us (2%)
    unnamed x3, waiting for transfers between devices  93.4 us
    psum x1, waiting for transfers between devices, body(): lax.psum((proj_part, gain_part, bias_part), 'dp')  83.4 us
    all_gather x2, blocking collectives, fold_rows(): lax.all_gather(values, 'dp', axis=0, tiled=True)  46.8 us
    dot_general x2, matrix products, contract_rows(): lax.dot_general(left, right, (((0,), (0,)), ((), ())), preferred_element_...  18 us
    dot_general x2, matrix products, contract_last(): lax.dot_general(left, right, (((1,), (1,)), ((), ())), preferred_element_...  12.9 us
    unnamed x28, local copies, waits for them, and re-layouts  10.2 us
    all_to_all x1, starting transfers between devices, body(): lax.all_to_all(normed, 'dp', split_axis=1, concat_axis=0, tiled=True)  7.39 us
  transfers between devices with their start and end apart: 4, of which 3 were waited for; matrix products, arithmetic and copies ran while one was open for 9% of the time, Pallas kernels for 0%

commit v1 on v0

--- a/solution.py
+++ b/solution.py
@@ -1,6 +1,11 @@
+import functools
+import math
+
 import jax
 import jax.numpy as jnp
 from jax import lax
+from jax.experimental import pallas as pl
+from jax.experimental.pallas import tpu as pltpu
 from jax.sharding import PartitionSpec as P
 
 epsilon = 1e-05
@@ -79,7 +84,7 @@
     )
 
 
-def body(embeddings, projection, norm_gain, norm_bias, up_weight, up_bias, down_weight, cotangent):
+def plain_body(embeddings, projection, norm_gain, norm_bias, up_weight, up_bias, down_weight, cotangent):
     own_rows = embeddings.shape[0]
     interaction = jax.vmap(lambda sample: interact_row(sample, projection))(embeddings)
     standard, inv_scale = layer_norm(interaction)
@@ -143,6 +148,379 @@
         grad_bias,
         grad_up,
         grad_up_bias,
+        grad_down,
+    )
+
+
+MESH = pl.DeviceIdType.MESH
+
+
+def greet(n, me):
+    barrier = pltpu.get_barrier_semaphore()
+
+    def signal(step, carry):
+        peer = lax.rem(me + step, n)
+        pl.semaphore_signal(barrier, inc=1, device_id={"dp": peer}, device_id_type=MESH)
+        return carry
+
+    lax.fori_loop(1, n, signal, 0)
+    pl.semaphore_wait(barrier, n - 1)
+
+
+def remote(source, target, sent, arrived, peer):
+    return pltpu.make_async_remote_copy(
+        src_ref=source,
+        dst_ref=target,
+        send_sem=sent,
+        recv_sem=arrived,
+        device_id={"dp": peer},
+        device_id_type=MESH,
+    )
+
+
+class Exchange:
+    def __init__(self, n, me, source, target, sent, arrived, same=False):
+        self.n, self.me, self.source, self.target = n, me, source, target
+        self.sent, self.arrived, self.same = sent, arrived, same
+
+    def copy(self, peer, slot):
+        source = self.source if self.same else self.source.at[peer]
+        return remote(
+            source, self.target.at[slot], self.sent.at[peer], self.arrived.at[slot], peer
+        )
+
+    def send(self, peer):
+        self.copy(peer, self.me).start()
+
+    def receive(self, peer):
+        self.copy(peer, peer).wait_recv()
+
+    def each(self, step_fn):
+        def step(k, carry):
+            step_fn(lax.rem(self.me + k, self.n))
+            return carry
+
+        lax.fori_loop(1, self.n, step, 0)
+
+    def send_all(self):
+        self.each(self.send)
+
+    def receive_all(self):
+        self.each(lambda peer: self.receive(lax.rem(2 * self.me + self.n - peer, self.n)))
+
+    def finish(self):
+        self.each(lambda peer: self.copy(peer, self.me).wait_send())
+
+
+def mlp_kernel(
+    n,
+    standard_ref,
+    gain_ref,
+    bias_ref,
+    up_bias_ref,
+    cot_ref,
+    up_hbm,
+    down_hbm,
+    out_ref,
+    columns_ref,
+    hidden_ref,
+    grad_preact_ref,
+    up_bias_grad_ref,
+    back_ref,
+    sums_ref,
+    up_ref,
+    down_ref,
+    std_in,
+    std_rows,
+    gh_send,
+    gh_recv,
+    pre_send,
+    pre_recv,
+    act_all,
+    back_send,
+    sums_own,
+    out_acc,
+    back_acc,
+    up_sem,
+    down_sem,
+    std_ss,
+    std_rs,
+    gh_ss,
+    gh_rs,
+    pre_ss,
+    pre_rs,
+    act_ss,
+    act_rs,
+    back_ss,
+    back_rs,
+    sums_ss,
+    sums_rs,
+):
+    me = lax.axis_index("dp")
+    own = standard_ref.shape[1]
+    rows = cot_ref.shape[0]
+    width = up_ref.shape[2]
+
+    def up_copy(j):
+        start = pl.multiple_of(j * width, width)
+        return pltpu.make_async_copy(up_hbm.at[:, pl.ds(start, width)], up_ref.at[j], up_sem.at[j])
+
+    def down_copy(j):
+        start = pl.multiple_of(j * width, width)
+        return pltpu.make_async_copy(
+            down_hbm.at[pl.ds(start, width), :], down_ref.at[j], down_sem.at[j]
+        )
+
+    def loop(step_fn):
+        def step(k, carry):
+            step_fn(lax.rem(me + k, n))
+            return carry
+
+        lax.fori_loop(1, n + 1, step, 0)
+
+    loop(lambda j: down_copy(j).start())
+    loop(lambda j: up_copy(j).start())
+    greet(n, me)
+
+    std = Exchange(n, me, standard_ref, std_in, std_ss, std_rs)
+    gh = Exchange(n, me, gh_send, gh_recv, gh_ss, gh_rs)
+    pre = Exchange(n, me, pre_send, pre_recv, pre_ss, pre_rs)
+    act = Exchange(n, me, act_all.at[me], act_all, act_ss, act_rs, same=True)
+    back = Exchange(n, me, back_send, back_ref, back_ss, back_rs)
+    sums = Exchange(n, me, sums_own, sums_ref, sums_ss, sums_rs, same=True)
+
+    std.send_all()
+    std_in[me] = standard_ref[me]
+
+    def hidden_step(j):
+        down_copy(j).wait()
+        part = lax.dot_general(
+            cot_ref[...], down_ref[j], (((1,), (1,)), ((), ())), preferred_element_type=jnp.float32
+        ).astype(jnp.bfloat16)
+
+        @pl.when(j != me)
+        def _():
+            gh_send[j] = part
+            gh.send(j)
+
+        @pl.when(j == me)
+        def _():
+            gh_recv[me] = part
+
+    loop(hidden_step)
+
+    std.receive_all()
+    for j in range(n):
+        std_rows[own * j : own * (j + 1), :] = std_in[j].astype(jnp.float32)
+    columns_ref[...] = (std_rows[...] * gain_ref[me] + bias_ref[me]).astype(jnp.bfloat16)
+
+    def preact_step(j):
+        up_copy(j).wait()
+        part = jnp.dot(
+            columns_ref[...], up_ref[j], preferred_element_type=jnp.float32
+        ).astype(jnp.bfloat16)
+
+        @pl.when(j != me)
+        def _():
+            pre_send[j] = part
+            pre.send(j)
+
+        @pl.when(j == me)
+        def _():
+            pre_recv[me] = part
+
+    loop(preact_step)
+
+    gh.receive_all()
+    grad_hidden = gh_recv[0].astype(jnp.float32)
+    for j in range(1, n):
+        grad_hidden = grad_hidden + gh_recv[j].astype(jnp.float32)
+    pre.receive_all()
+    preact = pre_recv[0].astype(jnp.float32)
+    for j in range(1, n):
+        preact = preact + pre_recv[j].astype(jnp.float32)
+    preact = preact + up_bias_ref[me]
+    root = math.sqrt(2 / math.pi)
+    square = preact * preact
+    bent = jnp.tanh(root * preact * (1.0 + 0.044715 * square))
+    half = 0.5 * (1.0 + bent)
+    slope = half + 0.5 * preact * (1.0 - bent * bent) * (root * (1.0 + 3 * 0.044715 * square))
+    act_all[me, 0] = (preact * half).astype(jnp.bfloat16)
+    act_all[me, 1] = (grad_hidden * slope).astype(jnp.bfloat16)
+    act.send_all()
+
+    def gather_step(j):
+        columns = pl.ds(pl.multiple_of(j * width, width), width)
+        hidden = act_all[j, 0]
+        grad = act_all[j, 1]
+        hidden_ref[:, columns] = hidden
+        grad_preact_ref[:, columns] = grad
+        up_bias_grad_ref[:, columns] = jnp.sum(grad.astype(jnp.float32), axis=0, keepdims=True)
+        out_acc[...] += jnp.dot(hidden, down_ref[j], preferred_element_type=jnp.float32)
+        back_acc[...] += lax.dot_general(
+            grad, up_ref[j], (((1,), (1,)), ((), ())), preferred_element_type=jnp.float32
+        )
+
+    out_acc[...] = jnp.zeros_like(out_acc)
+    back_acc[...] = jnp.zeros_like(back_acc)
+    gather_step(me)
+
+    def arrive_step(k, carry):
+        j = lax.rem(me + n - k, n)
+        act.receive(j)
+        gather_step(j)
+        return carry
+
+    lax.fori_loop(1, n, arrive_step, 0)
+
+    grad_normed = back_acc[...].astype(jnp.bfloat16)
+    wide = grad_normed.astype(jnp.float32)
+    back_acc[...] = wide
+    for j in range(n):
+        back_send[j] = back_acc[own * j : own * (j + 1), :].astype(jnp.bfloat16)
+    back.send_all()
+    back_ref[me] = back_send[me]
+    sums_own[0:1, :] = jnp.sum(wide * std_rows[...], axis=0, keepdims=True)
+    sums_own[1:2, :] = jnp.sum(wide, axis=0, keepdims=True)
+    sums.send_all()
+    sums_ref[me] = sums_own[...]
+    out_ref[...] = out_acc[...].astype(jnp.bfloat16)
+    for exchange in (std, gh, pre, act):
+        exchange.finish()
+    back.receive_all()
+    sums.receive_all()
+    back.finish()
+    sums.finish()
+
+
+def mlp(standard, norm_gain, norm_bias, up_weight, up_bias, down_weight, cotangent):
+    n = lax.axis_size("dp")
+    own = standard.shape[0]
+    rows, features = cotangent.shape
+    units = up_weight.shape[1]
+    width = units // n
+    blocks = jnp.swapaxes(standard.astype(jnp.bfloat16).reshape(own, n, features), 0, 1)
+    vmem = pl.BlockSpec(memory_space=pltpu.VMEM)
+    hbm = pl.BlockSpec(memory_space=pl.ANY)
+    bf16, f32 = jnp.bfloat16, jnp.float32
+    shape = jax.ShapeDtypeStruct
+    return pl.pallas_call(
+        functools.partial(mlp_kernel, n),
+        out_shape=(
+            shape((rows, features), bf16),
+            shape((rows, features), bf16),
+            shape((rows, units), bf16),
+            shape((rows, units), bf16),
+            shape((1, units), f32),
+            shape((n, own, features), bf16),
+            shape((n, 2, features), f32),
+        ),
+        in_specs=[vmem] * 5 + [hbm] * 2,
+        out_specs=[vmem] * 7,
+        scratch_shapes=[
+            pltpu.VMEM((n, features, width), bf16),
+            pltpu.VMEM((n, width, features), bf16),
+            pltpu.VMEM((n, own, features), bf16),
+            pltpu.VMEM((rows, features), f32),
+            pltpu.VMEM((n, rows, width), bf16),
+            pltpu.VMEM((n, rows, width), bf16),
+            pltpu.VMEM((n, rows, width), bf16),
+            pltpu.VMEM((n, rows, width), bf16),
+            pltpu.VMEM((n, 2, rows, width), bf16),
+            pltpu.VMEM((n, own, features), bf16),
+            pltpu.VMEM((2, features), f32),
+            pltpu.VMEM((rows, features), f32),
+            pltpu.VMEM((rows, features), f32),
+        ]
+        + [pltpu.SemaphoreType.DMA((n,))] * 14,
+        compiler_params=pltpu.CompilerParams(
+            collective_id=0, has_side_effects=True, vmem_limit_bytes=48 * 2**20
+        ),
+        cost_estimate=pl.CostEstimate(
+            flops=8 * rows * features * units,
+            bytes_accessed=4 * features * units,
+            transcendentals=rows * width,
+        ),
+        name="perceptron",
+    )(
+        blocks,
+        norm_gain.reshape(n, 1, features),
+        norm_bias.reshape(n, 1, features),
+        up_bias.reshape(n, 1, width),
+        cotangent,
+        up_weight,
+        down_weight,
+    )
+
+
+def total_kernel(n, part_ref, total_ref, parts, own_total, part_ss, part_rs, total_ss, total_rs):
+    me = lax.axis_index("dp")
+    greet(n, me)
+    first = Exchange(n, me, part_ref, parts, part_ss, part_rs)
+    second = Exchange(n, me, own_total, total_ref, total_ss, total_rs, same=True)
+    first.send_all()
+    parts[me] = part_ref[me]
+    first.receive_all()
+    total = parts[0]
+    for j in range(1, n):
+        total = total + parts[j]
+    own_total[...] = total
+    second.send_all()
+    total_ref[me] = total
+    first.finish()
+    second.receive_all()
+    second.finish()
+
+
+def total_over_rows(part):
+    n = lax.axis_size("dp")
+    height, width = part.shape
+    vmem = pl.BlockSpec(memory_space=pltpu.VMEM)
+    blocks = (n, height // n, width)
+    total = pl.pallas_call(
+        functools.partial(total_kernel, n),
+        out_shape=jax.ShapeDtypeStruct(blocks, jnp.float32),
+        in_specs=[vmem],
+        out_specs=vmem,
+        scratch_shapes=[
+            pltpu.VMEM(blocks, jnp.float32),
+            pltpu.VMEM(blocks[1:], jnp.float32),
+        ]
+        + [pltpu.SemaphoreType.DMA((n,))] * 4,
+        compiler_params=pltpu.CompilerParams(collective_id=1, has_side_effects=True),
+        name="total",
+    )(part.reshape(blocks))
+    return total.reshape(height, width)
+
+
+def body(embeddings, projection, norm_gain, norm_bias, up_weight, up_bias, down_weight, cotangent):
+    n = lax.axis_size("dp")
+    own_rows = embeddings.shape[0]
+    if (up_weight.shape[1] // n) % 128 or cotangent.shape[0] % 16:
+        return plain_body(
+            embeddings, projection, norm_gain, norm_bias, up_weight, up_bias, down_weight, cotangent
+        )
+    interaction = jax.vmap(lambda sample: interact_row(sample, projection))(embeddings)
+    standard, inv_scale = layer_norm(interaction)
+    out, columns, hidden, grad_preact, grad_up_bias, back, sums = mlp(
+        standard, norm_gain, norm_bias, up_weight, up_bias, down_weight, cotangent
+    )
+    grad_up = contract_rows(columns, grad_preact)
+    grad_down = contract_rows(hidden, cotangent)
+    grad_normed = jnp.swapaxes(back, 0, 1).reshape(own_rows, -1).astype(jnp.float32)
+    grad_interaction = norm_back(grad_normed, standard, inv_scale, norm_gain).astype(jnp.bfloat16)
+    grad_embeddings, proj_rows = jax.vmap(
+        lambda sample, grad_flat: interact_back(sample, projection, grad_flat)
+    )(embeddings, grad_interaction)
+    grad_projection = total_over_rows(jnp.sum(proj_rows, axis=0))
+    return (
+        out,
+        grad_embeddings,
+        grad_projection,
+        sums[:, 0, :].reshape(-1),
+        sums[:, 1, :].reshape(-1),
+        grad_up,
+        grad_up_bias.reshape(-1),
         grad_down,
     )
 

time: 326 us -> 116 us (0.36)
  waiting for transfers between devices: 178 us -> 0 us
  Pallas kernels: 0 us -> 75.8 us
  blocking collectives: 46.8 us -> 0 us
  matrix products: 52.6 us -> 24.5 us
  between operations: 14.9 us -> 0.87 us
  starting transfers between devices: 11.6 us -> 0 us
  local copies, waits for them, and re-layouts: 15.6 us -> 11.4 us
  other arithmetic: 6.1 us -> 2.68 us
    unnamed x3 -> x0, waiting for transfers between devices: 93.4 us -> none
    psum x1 -> x0, waiting for transfers between devices: 83.4 us -> none  [body(): lax.psum((proj_part, gain_part, bias_part), 'dp')]
    pallas_call x0 -> x2, Pallas kernels: none -> 75.8 us  [the longest x1 58.8 us: mlp(): pl.pallas_call(functools.partial(mlp_kernel, n), out_shape=(shape((rows,...]
    all_gather x2 -> x0, blocking collectives: 46.8 us -> none  [fold_rows(): lax.all_gather(values, 'dp', axis=0, tiled=True)]
    dot_general x4 -> x0, matrix products: 24.3 us -> none  [the longest x2 12.9 us: contract_last(): lax.dot_general(left, right, (((1,), (1,)), ((), ())), preferred_element_...]
    all_to_all x2 -> x0, starting transfers between devices: 11.6 us -> none  [the longest x1 7.39 us: body(): lax.all_to_all(normed, 'dp', split_axis=1, concat_axis=0, tiled=True)]
    unnamed x28 -> x33, local copies, waits for them, and re-layouts: 10.2 us -> 3.39 us
    convert_element_type x3, local copies, waits for them, and re-layouts: 1.01 us -> 4.4 us  [body(): jnp.swapaxes(back, 0, 1).reshape(own_rows, -1).astype(jnp.float32)]
  transfers between devices with their start and end apart: 4 -> 0, of which waited for: 3 -> 0; matrix products, arithmetic and copies ran while one was open for 9% -> 0% of each run, Pallas kernels for 0% -> 0%
where the time goes in v1:
time: 116 us; the launch traced here: 115 us
  Pallas kernels  75.8 us (65%)
  matrix products  24.5 us (21%)
  local copies, waits for them, and re-layouts  11.4 us (10%)
  other arithmetic  2.68 us (2%)
    pallas_call x1, Pallas kernels, mlp(): pl.pallas_call(functools.partial(mlp_kernel, n), out_shape=(shape((rows,...  58.8 us
    dot_general x2, matrix products, contract_rows(): lax.dot_general(left, right, (((0,), (0,)), ((), ())), preferred_element_...  17.1 us
    pallas_call x1, Pallas kernels, total_over_rows(): pl.pallas_call(functools.partial(total_kernel, n), out_shape=jax.ShapeDty...  16.9 us
    convert_element_type x3, local copies, waits for them, and re-layouts, body(): jnp.swapaxes(back, 0, 1).reshape(own_rows, -1).astype(jnp.float32)  4.4 us
    unnamed x33, local copies, waits for them, and re-layouts  3.39 us
    mul x3, local copies, waits for them, and re-layouts, norm_back(): scaled = grad_normed * norm_gain  2.57 us

profile of v1, /device:TPU:0, one launch (start us, length us, event | category | flops | bytes accessed | tf_op | source)
XLA Modules:
  0.0 115.2 jit_solution(16425627509167598719)
XLA Ops:
  0.6 0.0 copy-start
  0.6 0.9 mul.68
  1.6 0.9 mul.65
  2.5 0.7 copy.22
  3.2 0.0 copy-done
  3.2 0.0 copy-start.11
  3.2 0.6 convolution_convert_fusion.1
  3.8 0.2 copy-done.11
  4.1 0.0 copy-start.5
  4.1 0.6 convolution_convert_fusion.2
  4.7 0.0 copy-start.8
  4.7 0.0 copy-start.1
  4.7 0.0 copy-start.2
  4.7 0.0 copy-start.3
  4.7 0.0 copy-start.4
  4.7 0.4 fusion.11
  5.1 0.0 copy-start.7
  5.1 0.0 copy-start.13
  5.1 0.2 multiply_reduce_fusion
  5.3 0.0 copy-done.5
  5.3 0.0 copy-start.14
  5.3 0.2 copy.19
  5.5 0.2 reshape.129
  5.6 0.0 copy-done.8
  5.6 0.1 copy-done.7
  5.8 0.2 fusion.7.standard_ref
  5.9 0.0 copy-done.1
  5.9 0.0 copy-done.2
  5.9 0.0 copy-done.3
  5.9 0.0 copy-done.4
  6.0 58.8 %perceptron.1 = (bf16[48,1024]{1,0:T(8,128)(2,1)S(1)}, bf16[48,1024]{1,0:T(8,128)(2,1)S(1)}, bf16[48,4096]{1,0:T(8,128)(2,1)S(1)}, bf16[48,4096]{1,0:T(8,128)(2,...) custom-call(bf16[16,3,1024]{2,1,0:T(4,128)(2,1)S(1)} %fusion.7.standard_ref, ...), custom_call_target="tpu_custom_call" | custom-call | flops 1610612736 | bytes 16777216 | tf_op jit(solution)/shard_map/perceptron/pallas_call | solution.py:407
  64.8 0.0 copy-done.13
  64.8 0.0 copy-done.14
  64.8 0.3 fusion.4
  65.2 0.3 fusion.2
  65.4 0.5 broadcast_multiply_fusion
  65.9 0.8 fusion.10
  66.7 0.0 copy-start.6
  66.7 0.8 copy.21
  67.5 1.8 %reshape.136 = f32[3,256,64]{2,1,0:T(8,128)} reshape(f32[3,16,1024]{2,1,0:T(8,128)} %copy.21) | data formatting | bytes 393216 | tf_op jit(solution)/shard_map/convert_element_type | solution.py:510
  69.3 1.8 %copy.23 = f32[3,256,64]{1,2,0:T(8,128)} copy(f32[3,256,64]{2,1,0:T(8,128)} %reshape.136) | data formatting | bytes 393216 | tf_op jit(solution)/shard_map/convert_element_type | solution.py:510
  71.1 1.2 %multiply_convert_fusion = bf16[3,256,64]{1,2,0:T(8,128)(2,1)S(1)} fusion(f32[3,256,64]{1,2,0:T(8,128)} %copy.23, f32[3]{0:T(128)} %get-tuple-element.42, f32[3]{0:T(128)} %get-tuple-element.43, f32[256,64]{0,1:T(8,128)} %copy.22, f32[3]{0:T(128)} %copy-done.14, f32[3]{0:T(128)} %copy-done.13, f32[3,64,256]{2,1,0:T(8,128)} %copy-done.7), kind=kLoop, calls=%fused_computation.15 | loop fusion | flops 393216 | bytes 557104 | tf_op jit(solution)/shard_map/convert_element_type | solution.py:511
  72.3 0.4 fusion
  72.7 0.0 copy-done.6
  72.7 0.0 copy-start.9
  72.7 1.3 %fusion.14 = f32[512,64,1]{1,0,2:T(8,128)} fusion(bf16[3,512,512]{2,1,0:T(8,128)(2,1)S(1)} %copy-done.6, bf16[3,512,64]{1,2,0:T(8,128)(2,1)S(1)} %fusion), kind=kOutput, calls=%fused_computation.28 | convolution fusion | flops 100663296 | bytes 1900544 | tf_op jit(solution)/shard_map/vmap()/dot_general | solution.py:47
  74.0 0.0 copy-done.9
  74.0 0.0 copy-start.12
  74.0 0.0 copy-start.10
  74.0 16.9 %total.1 = f32[16,32,64]{2,1,0:T(8,128)} custom-call(f32[16,32,64]{2,1,0:T(8,128)} %bitcast.56), custom_call_target="tpu_custom_call" | custom-call | tf_op jit(solution)/shard_map/total/pallas_call | solution.py:480
  91.0 1.7 %copy.26 = f32[512,64]{0,1:T(8,128)} copy(f32[512,64]{1,0:T(8,128)} %bitcast.55) | data formatting | bytes 262144
  92.7 1.3 %fusion.12 = f32[3,512,256]{2,1,0:T(8,128)S(1)} fusion(bf16[3,512,64]{1,2,0:T(8,128)(2,1)} %copy-done.8, bf16[3,256,64]{1,2,0:T(8,128)(2,1)S(1)} %multiply_convert_fusion), kind=kOutput, calls=%fused_computation.26 | convolution fusion | flops 50331648 | bytes 1867776 | tf_op jit(solution)/shard_map/vmap()/dot_general | solution.py:41
  94.0 0.0 copy-done.12
  94.0 0.0 copy-done.10
  94.0 0.6 convolution_convert_fusion
  94.6 0.6 fusion.13
  95.2 1.7 %add_convert_fusion = bf16[3,512,256]{2,1,0:T(8,128)(2,1)} fusion(f32[3,512,256]{2,1,0:T(8,128)S(1)} %fusion.12, f32[3,512,256]{2,1,0:T(8,128)S(1)} %fusion.13, bf16[3,512,512]{2,1,0:T(8,128)(2,1)S(1)} %convolution_convert_fusion, bf16[3,512,256]{2,1,0:T(8,128)(2,1)S(1)} %copy-done), kind=kOutput, calls=%fused_computation.2 | convolution fusion | flops 403832832 | bytes 6291456 | tf_op jit(solution)/shard_map/vmap()/dot_general | solution.py:46
  96.9 8.5 %fusion.15 = f32[1024,4096]{1,0:T(8,128)} fusion(bf16[48,1024]{1,0:T(8,128)(2,1)S(1)} %get-tuple-element.18, bf16[48,4096]{1,0:T(8,128)(2,1)S(1)} %get-tuple-element.19), kind=kOutput, calls=%fused_computation.29 | convolution fusion | flops 402653184 | bytes 17268736 | tf_op jit(solution)/shard_map/dot_general | solution.py:76
  105.5 8.5 %fusion.16 = f32[4096,1024]{1,0:T(8,128)} fusion(bf16[48,4096]{1,0:T(8,128)(2,1)S(1)} %get-tuple-element.21, bf16[48,1024]{1,0:T(8,128)(2,1)S(1)} %copy-done.2), kind=kOutput, calls=%fused_computation.30 | convolution fusion | flops 402653184 | bytes 17268736 | tf_op jit(solution)/shard_map/dot_general | solution.py:76
  114.0 0.6 copy.41
  114.6 0.6 copy.42
  (3 shorter events, 0.0 us)
Async XLA Ops:
  0.6 2.6 %copy-start = (bf16[3,512,256]{2,1,0:T(8,128)(2,1)S(1)}, bf16[3,512,256]{2,1,0:T(8,128)(2,1)}, u32[]{:S(2)}) copy-start(bf16[3,512,256]{2,1,0:T(8,128)(2,1)} %param.8) | copy-start | bytes 2359300
  3.2 0.8 copy-start.11
  4.1 1.2 %copy-start.5 = (bf16[3,512,512]{2,1,0:T(8,128)(2,1)}, bf16[3,512,512]{2,1,0:T(8,128)(2,1)S(1)}, u32[]{:S(2)}) copy-start(bf16[3,512,512]{2,1,0:T(8,128)(2,1)S(1)} %convolution_convert_fusion.1) | copy-start | bytes 4718596
  4.7 1.0 copy-start.8
  4.7 1.2 %copy-start.1 = (f32[16384]{0:T(1024)S(1)}, f32[16384]{0:T(1024)}, u32[]{:S(2)}) copy-start(f32[16384]{0:T(1024)} %param.10) | copy-start | bytes 196612
  4.7 1.2 %copy-start.2 = (bf16[48,1024]{1,0:T(8,128)(2,1)S(1)}, bf16[48,1024]{1,0:T(8,128)(2,1)}, u32[]{:S(2)}) copy-start(bf16[48,1024]{1,0:T(8,128)(2,1)} %cot_ref.1) | copy-start | bytes 294916
  4.7 1.2 %copy-start.3 = (f32[16384]{0:T(1024)S(1)}, f32[16384]{0:T(1024)}, u32[]{:S(2)}) copy-start(f32[16384]{0:T(1024)} %param.11) | copy-start | bytes 196612
  4.7 1.2 %copy-start.4 = (f32[4096]{0:T(1024)S(1)}, f32[4096]{0:T(1024)}, u32[]{:S(2)}) copy-start(f32[4096]{0:T(1024)} %param.13) | copy-start | bytes 49156
  5.1 0.7 copy-start.7
  5.1 59.7 %copy-start.13 = (f32[3]{0:T(128)}, f32[3]{0:T(128)S(1)}, u32[]{:S(2)}) copy-start(f32[3]{0:T(128)S(1)} %broadcast_multiply_fusion.2) | copy-start | bytes 40
  5.3 59.5 %copy-start.14 = (f32[3]{0:T(128)}, f32[3]{0:T(128)S(1)}, u32[]{:S(2)}) copy-start(f32[3]{0:T(128)S(1)} %add_rsqrt_fusion) | copy-start | bytes 40
  66.7 6.0 %copy-start.6 = (bf16[3,512,512]{2,1,0:T(8,128)(2,1)S(1)}, bf16[3,512,512]{2,1,0:T(8,128)(2,1)}, u32[]{:S(2)}) copy-start(bf16[3,512,512]{2,1,0:T(8,128)(2,1)} %copy-done.5) | copy-start | bytes 4718596
  72.7 1.3 %copy-start.9 = (bf16[3,512,64]{1,2,0:T(8,128)(2,1)}, bf16[3,512,64]{1,2,0:T(8,128)(2,1)S(1)}, u32[]{:S(2)}) copy-start(bf16[3,512,64]{1,2,0:T(8,128)(2,1)S(1)} %fusion) | copy-start | bytes 589828
  74.0 20.0 %copy-start.12 = (bf16[512,64]{0,1:T(8,128)(2,1)S(1)}, bf16[512,64]{0,1:T(8,128)(2,1)}, u32[]{:S(2)}) copy-start(bf16[512,64]{0,1:T(8,128)(2,1)} %param.9) | copy-start | bytes 196612
  74.0 20.0 %copy-start.10 = (bf16[3,512,64]{1,2,0:T(8,128)(2,1)S(1)}, bf16[3,512,64]{1,2,0:T(8,128)(2,1)}, u32[]{:S(2)}) copy-start(bf16[3,512,64]{1,2,0:T(8,128)(2,1)} %copy-done.9) | copy-start | bytes 589828

commit v2 on v1

--- a/solution.py
+++ b/solution.py
@@ -164,7 +164,7 @@
         return carry
 
     lax.fori_loop(1, n, signal, 0)
-    pl.semaphore_wait(barrier, n - 1)
+    return lambda: pl.semaphore_wait(barrier, n - 1)
 
 
 def remote(source, target, sent, arrived, peer):
@@ -214,7 +214,8 @@
 
 def mlp_kernel(
     n,
-    standard_ref,
+    emb_ref,
+    proj_ref,
     gain_ref,
     bias_ref,
     up_bias_ref,
@@ -226,8 +227,20 @@
     hidden_ref,
     grad_preact_ref,
     up_bias_grad_ref,
+    grad_emb_ref,
+    grad_proj_ref,
+    sums_ref,
+    pairs,
+    compressed,
+    folded,
+    standard,
+    standard_ref,
+    gain_rows,
     back_ref,
-    sums_ref,
+    grad_rows,
+    part_send,
+    part_recv,
+    own_total,
     up_ref,
     down_ref,
     std_in,
@@ -255,9 +268,16 @@
     back_rs,
     sums_ss,
     sums_rs,
+    part_ss,
+    part_rs,
+    total_ss,
+    total_rs,
 ):
     me = lax.axis_index("dp")
-    own = standard_ref.shape[1]
+    own = emb_ref.shape[0]
+    columns_k = proj_ref.shape[1]
+    stride = cot_ref.shape[1] // columns_k
+    count = n * cot_ref.shape[1]
     rows = cot_ref.shape[0]
     width = up_ref.shape[2]
 
@@ -280,7 +300,36 @@
 
     loop(lambda j: down_copy(j).start())
     loop(lambda j: up_copy(j).start())
-    greet(n, me)
+    await_peers = greet(n, me)
+
+    def whole_sum(values):
+        return jnp.sum(jnp.sum(values, axis=1, keepdims=True), axis=0, keepdims=True)
+
+    inv_scales = []
+    for b in range(own):
+        sample = emb_ref[b]
+        pairs[b] = lax.dot_general(
+            sample, sample, (((1,), (1,)), ((), ())), preferred_element_type=jnp.float32
+        ).astype(jnp.bfloat16)
+        compressed[b] = jnp.dot(
+            pairs[b], proj_ref[...], preferred_element_type=jnp.float32
+        ).astype(jnp.bfloat16)
+        interaction = lax.dot_general(
+            sample, compressed[b], (((0,), (0,)), ((), ())), preferred_element_type=jnp.float32
+        )
+        centre = interaction - whole_sum(interaction) / count
+        inv_scale = lax.rsqrt(whole_sum(centre * centre) / count + epsilon)
+        inv_scales.append(inv_scale)
+        folded[b] = centre * inv_scale
+        for m in range(0, stride, 2):
+            standard[b, :, columns_k * m : columns_k * (m + 2)] = jnp.concatenate(
+                [folded[b, pl.ds(m, n, stride=stride), :], folded[b, pl.ds(m + 1, n, stride=stride), :]],
+                axis=1,
+            )
+    for j in range(n):
+        standard_ref[j] = standard[:, j, :].astype(jnp.bfloat16)
+        gain_rows[j : j + 1, :] = gain_ref[j]
+    await_peers()
 
     std = Exchange(n, me, standard_ref, std_in, std_ss, std_rs)
     gh = Exchange(n, me, gh_send, gh_recv, gh_ss, gh_rs)
@@ -387,19 +436,66 @@
     out_ref[...] = out_acc[...].astype(jnp.bfloat16)
     for exchange in (std, gh, pre, act):
         exchange.finish()
+    part = Exchange(n, me, part_send, part_recv, part_ss, part_rs)
+    total = Exchange(n, me, own_total, grad_proj_ref, total_ss, total_rs, same=True)
     back.receive_all()
+    for j in range(n):
+        grad_rows[:, j, :] = back_ref[j].astype(jnp.float32)
+    proj_part = None
+    saved = []
+    for b in range(own):
+        scaled = grad_rows[b] * gain_rows[...]
+        first = whole_sum(scaled) / count
+        second = whole_sum(scaled * standard[b]) / count
+        grads = inv_scales[b] * (scaled - first - standard[b] * second)
+        for m in range(stride):
+            folded[b, pl.ds(m, n, stride=stride), :] = grads[:, columns_k * m : columns_k * (m + 1)]
+        grad_matrix = folded[b].astype(jnp.bfloat16)
+        grad_compressed = jnp.dot(
+            emb_ref[b], grad_matrix, preferred_element_type=jnp.float32
+        ).astype(jnp.bfloat16)
+        saved.append((grad_matrix, grad_compressed))
+        term = jnp.dot(pairs[b], grad_compressed, preferred_element_type=jnp.float32)
+        proj_part = term if proj_part is None else proj_part + term
+    part_send[...] = proj_part.reshape(part_send.shape)
+    part.send_all()
+    part_recv[me] = part_send[me]
+    for b in range(own):
+        grad_matrix, grad_compressed = saved[b]
+        last = (((1,), (1,)), ((), ()))
+        grad_pairs = lax.dot_general(
+            grad_compressed, proj_ref[...], last, preferred_element_type=jnp.float32
+        ).astype(jnp.bfloat16)
+        turned = lax.dot_general(
+            proj_ref[...], grad_compressed, last, preferred_element_type=jnp.float32
+        ).astype(jnp.bfloat16)
+        grad_sample = lax.dot_general(
+            compressed[b], grad_matrix, last, preferred_element_type=jnp.float32
+        )
+        grad_sample += jnp.dot(grad_pairs, emb_ref[b], preferred_element_type=jnp.float32)
+        grad_sample += jnp.dot(turned, emb_ref[b], preferred_element_type=jnp.float32)
+        grad_emb_ref[b] = grad_sample.astype(jnp.bfloat16)
+        if b == 0:
+            part.receive_all()
+            whole = part_recv[0]
+            for j in range(1, n):
+                whole = whole + part_recv[j]
+            own_total[...] = whole
+            total.send_all()
+            grad_proj_ref[me] = whole
     sums.receive_all()
-    back.finish()
-    sums.finish()
-
-
-def mlp(standard, norm_gain, norm_bias, up_weight, up_bias, down_weight, cotangent):
+    total.receive_all()
+    for exchange in (back, sums, part, total):
+        exchange.finish()
+
+
+def mlp(embeddings, projection, norm_gain, norm_bias, up_weight, up_bias, down_weight, cotangent):
     n = lax.axis_size("dp")
-    own = standard.shape[0]
+    own, samples, depth = embeddings.shape
+    kept = projection.shape[1]
     rows, features = cotangent.shape
     units = up_weight.shape[1]
     width = units // n
-    blocks = jnp.swapaxes(standard.astype(jnp.bfloat16).reshape(own, n, features), 0, 1)
     vmem = pl.BlockSpec(memory_space=pltpu.VMEM)
     hbm = pl.BlockSpec(memory_space=pl.ANY)
     bf16, f32 = jnp.bfloat16, jnp.float32
@@ -412,12 +508,24 @@
             shape((rows, units), bf16),
             shape((rows, units), bf16),
             shape((1, units), f32),
-            shape((n, own, features), bf16),
+            shape(embeddings.shape, bf16),
+            shape((n, samples // n, kept), f32),
             shape((n, 2, features), f32),
         ),
-        in_specs=[vmem] * 5 + [hbm] * 2,
-        out_specs=[vmem] * 7,
+        in_specs=[vmem] * 6 + [hbm] * 2,
+        out_specs=[vmem] * 8,
         scratch_shapes=[
+            pltpu.VMEM((own, samples, samples), bf16),
+            pltpu.VMEM((own, samples, kept), bf16),
+            pltpu.VMEM((own, depth, kept), f32),
+            pltpu.VMEM((own, n, features), f32),
+            pltpu.VMEM((n, own, features), bf16),
+            pltpu.VMEM((n, features), f32),
+            pltpu.VMEM((n, own, features), bf16),
+            pltpu.VMEM((own, n, features), f32),
+            pltpu.VMEM((n, samples // n, kept), f32),
+            pltpu.VMEM((n, samples // n, kept), f32),
+            pltpu.VMEM((samples // n, kept), f32),
             pltpu.VMEM((n, features, width), bf16),
             pltpu.VMEM((n, width, features), bf16),
             pltpu.VMEM((n, own, features), bf16),
@@ -432,7 +540,7 @@
             pltpu.VMEM((rows, features), f32),
             pltpu.VMEM((rows, features), f32),
         ]
-        + [pltpu.SemaphoreType.DMA((n,))] * 14,
+        + [pltpu.SemaphoreType.DMA((n,))] * 18,
         compiler_params=pltpu.CompilerParams(
             collective_id=0, has_side_effects=True, vmem_limit_bytes=48 * 2**20
         ),
@@ -443,7 +551,8 @@
         ),
         name="perceptron",
     )(
-        blocks,
+        embeddings,
+        projection,
         norm_gain.reshape(n, 1, features),
         norm_bias.reshape(n, 1, features),
         up_bias.reshape(n, 1, width),
@@ -453,44 +562,39 @@
     )
 
 
-def total_kernel(n, part_ref, total_ref, parts, own_total, part_ss, part_rs, total_ss, total_rs):
-    me = lax.axis_index("dp")
-    greet(n, me)
-    first = Exchange(n, me, part_ref, parts, part_ss, part_rs)
-    second = Exchange(n, me, own_total, total_ref, total_ss, total_rs, same=True)
-    first.send_all()
-    parts[me] = part_ref[me]
-    first.receive_all()
-    total = parts[0]
-    for j in range(1, n):
-        total = total + parts[j]
-    own_total[...] = total
-    second.send_all()
-    total_ref[me] = total
-    first.finish()
-    second.receive_all()
-    second.finish()
-
-
-def total_over_rows(part):
-    n = lax.axis_size("dp")
-    height, width = part.shape
-    vmem = pl.BlockSpec(memory_space=pltpu.VMEM)
-    blocks = (n, height // n, width)
-    total = pl.pallas_call(
-        functools.partial(total_kernel, n),
-        out_shape=jax.ShapeDtypeStruct(blocks, jnp.float32),
-        in_specs=[vmem],
-        out_specs=vmem,
-        scratch_shapes=[
-            pltpu.VMEM(blocks, jnp.float32),
-            pltpu.VMEM(blocks[1:], jnp.float32),
-        ]
-        + [pltpu.SemaphoreType.DMA((n,))] * 4,
-        compiler_params=pltpu.CompilerParams(collective_id=1, has_side_effects=True),
-        name="total",
-    )(part.reshape(blocks))
-    return total.reshape(height, width)
+def weight_kernel(columns_ref, grad_preact_ref, hidden_ref, cot_ref, up_ref, down_ref):
+    up_ref[...] = contract_rows(columns_ref[...], grad_preact_ref[...])
+    down_ref[...] = contract_rows(hidden_ref[...], cot_ref[...])
+
+
+def weight_grads(columns, grad_preact, hidden, cotangent):
+    rows, features = columns.shape
+    units = hidden.shape[1]
+    steps = math.gcd(features, units) // 128
+    while steps > 16:
+        steps //= 2
+
+    def part(extent):
+        return pl.BlockSpec((rows, extent // steps), lambda i: (0, i))
+
+    def whole(extent):
+        return pl.BlockSpec((rows, extent), lambda i: (0, 0))
+
+    def result(height, width):
+        return pl.BlockSpec((height // steps, width), lambda i: (i, 0))
+
+    return pl.pallas_call(
+        weight_kernel,
+        grid=(steps,),
+        out_shape=(
+            jax.ShapeDtypeStruct((features, units), jnp.float32),
+            jax.ShapeDtypeStruct((units, features), jnp.float32),
+        ),
+        in_specs=[part(features), whole(units), part(units), whole(features)],
+        out_specs=(result(features, units), result(units, features)),
+        compiler_params=pltpu.CompilerParams(vmem_limit_bytes=40 * 2**20),
+        name="weight_grads",
+    )(columns, grad_preact, hidden, cotangent)
 
 
 def body(embeddings, projection, norm_gain, norm_bias, up_weight, up_bias, down_weight, cotangent):
@@ -500,23 +604,14 @@
         return plain_body(
             embeddings, projection, norm_gain, norm_bias, up_weight, up_bias, down_weight, cotangent
         )
-    interaction = jax.vmap(lambda sample: interact_row(sample, projection))(embeddings)
-    standard, inv_scale = layer_norm(interaction)
-    out, columns, hidden, grad_preact, grad_up_bias, back, sums = mlp(
-        standard, norm_gain, norm_bias, up_weight, up_bias, down_weight, cotangent
-    )
-    grad_up = contract_rows(columns, grad_preact)
-    grad_down = contract_rows(hidden, cotangent)
-    grad_normed = jnp.swapaxes(back, 0, 1).reshape(own_rows, -1).astype(jnp.float32)
-    grad_interaction = norm_back(grad_normed, standard, inv_scale, norm_gain).astype(jnp.bfloat16)
-    grad_embeddings, proj_rows = jax.vmap(
-        lambda sample, grad_flat: interact_back(sample, projection, grad_flat)
-    )(embeddings, grad_interaction)
-    grad_projection = total_over_rows(jnp.sum(proj_rows, axis=0))
+    out, columns, hidden, grad_preact, grad_up_bias, grad_embeddings, grad_projection, sums = mlp(
+        embeddings, projection, norm_gain, norm_bias, up_weight, up_bias, down_weight, cotangent
+    )
+    grad_up, grad_down = weight_grads(columns, grad_preact, hidden, cotangent)
     return (
         out,
         grad_embeddings,
-        grad_projection,
+        grad_projection.reshape(projection.shape),
         sums[:, 0, :].reshape(-1),
         sums[:, 1, :].reshape(-1),
         grad_up,

time: 116 us -> 95.1 us (0.82)
  matrix products: 24.5 us -> 0 us
  Pallas kernels: 75.8 us -> 85 us
  other arithmetic: 2.68 us -> 0 us
  local copies, waits for them, and re-layouts: 11.4 us -> 9.06 us
    dot_general x11 -> x0, matrix products: 24.5 us -> none  [the longest x2 17.1 us: contract_rows(): lax.dot_general(left, right, (((0,), (0,)), ((), ())), preferred_element_...]
    pallas_call x1, Pallas kernels: 58.8 us -> 73.6 us  [mlp(): pl.pallas_call(functools.partial(mlp_kernel, n), out_shape=(shape((rows,...]
    pallas_call x1, Pallas kernels: 16.9 us -> 11.4 us  [weight_grads(): pl.pallas_call(weight_kernel, grid=(steps,), out_shape=(jax.ShapeDtypeStr...]
    unnamed x33 -> x17, local copies, waits for them, and re-layouts: 3.39 us -> 8.31 us
    convert_element_type x3 -> x0, local copies, waits for them, and re-layouts: 4.4 us -> none  [body(): jnp.swapaxes(back, 0, 1).reshape(own_rows, -1).astype(jnp.float32)]
    mul x3 -> x0, local copies, waits for them, and re-layouts: 2.57 us -> none  [norm_back(): scaled = grad_normed * norm_gain]
    convert_element_type x2 -> x0, other arithmetic: 1.23 us -> none  [the longest x1 1.21 us: body(): norm_back(grad_normed, standard, inv_scale, norm_gain).astype(jnp.bfloat16)]
where the time goes in v2:
time: 95.1 us; the launch traced here: 94.8 us
  Pallas kernels  85 us (89%)
  local copies, waits for them, and re-layouts  9.06 us (10%)
    pallas_call x1, Pallas kernels, mlp(): pl.pallas_call(functools.partial(mlp_kernel, n), out_shape=(shape((rows,...  73.6 us
    pallas_call x1, Pallas kernels, weight_grads(): pl.pallas_call(weight_kernel, grid=(steps,), out_shape=(jax.ShapeDtypeStr...  11.4 us
    unnamed x17, local copies, waits for them, and re-layouts  8.31 us

profile of v2, /device:TPU:0, one launch (start us, length us, event | category | flops | bytes accessed | tf_op | source)
XLA Modules:
  0.0 94.8 jit_solution(1844860235860200532)
XLA Ops:
  0.6 0.0 copy-start.2
  0.6 1.0 %copy.16.proj_ref = bf16[512,64]{1,0:T(8,128)(2,1)S(1)} copy(bf16[512,64]{0,1:T(8,128)(2,1)} %param.9) | data formatting | bytes 131072 | tf_op args[1]
  1.6 0.0 copy-start
  1.7 1.1 %copy-done = bf16[3,512,256]{2,1,0:T(8,128)(2,1)S(1)} copy-done((bf16[3,512,256]{2,1,0:T(8,128)(2,1)S(1)}, bf16[3,512,256]{2,1,0:T(8,128)(2,1)}, u32[]{:S(2)}) %copy-start) | copy-done | bytes 786456
  2.8 0.0 copy-start.1
  2.8 0.9 copy-done.1
  3.7 0.0 copy-start.3
  3.7 0.8 copy-done.3
  4.5 0.0 copy-start.4
  4.5 0.8 copy-done.4
  5.4 0.0 copy-start.5
  5.4 0.7 copy-done.5
  6.1 73.6 %perceptron.1 = (bf16[48,1024]{1,0:T(8,128)(2,1)S(1)}, bf16[48,1024]{1,0:T(8,128)(2,1)S(1)}, bf16[48,4096]{1,0:T(8,128)(2,1)S(1)}, bf16[48,4096]{1,0:T(8,128)(2,...) custom-call(bf16[3,512,256]{2,1,0:T(8,128)(2,1)S(1)} %copy-done, ...), custom_call_target="tpu_custom_call" | custom-call | flops 1610612736 | bytes 16777216 | tf_op jit(solution)/shard_map/perceptron/pallas_call | solution.py:503
  79.7 0.8 copy.17
  80.5 0.8 fusion
  81.2 0.0 copy-done.2
  81.2 11.4 %weight_grads.1 = (f32[1024,4096]{1,0:T(8,128)}, f32[4096,1024]{1,0:T(8,128)}) custom-call(bf16[48,1024]{1,0:T(8,128)(2,1)S(1)} %get-tuple-element.22.columns_ref, bf16[48,4096]{1,0:T(8,128)(2,1)S(1)} %get-tuple-element.23.grad_preact_ref, bf16[48,4096]{1,0:T(8,128)(2,1)S(1)} %get-tuple-element.24.hidden_ref, bf16[48,1024]{1,0:T(8,128)(2,1)S(1)} %copy-done.2), custom_call_target="tpu_custom_call" | custom-call | tf_op jit(solution)/shard_map/weight_grads/pallas_call | solution.py:586
  92.6 0.6 copy.21
  93.3 0.9 copy.22
  94.1 0.6 copy.23
Async XLA Ops:
  0.6 80.6 %copy-start.2 = (bf16[48,1024]{1,0:T(8,128)(2,1)S(1)}, bf16[48,1024]{1,0:T(8,128)(2,1)}, u32[]{:S(2)}) copy-start(bf16[48,1024]{1,0:T(8,128)(2,1)} %cot_ref.3) | copy-start | bytes 294916
  1.6 1.1 %copy-start = (bf16[3,512,256]{2,1,0:T(8,128)(2,1)S(1)}, bf16[3,512,256]{2,1,0:T(8,128)(2,1)}, u32[]{:S(2)}) copy-start(bf16[3,512,256]{2,1,0:T(8,128)(2,1)} %emb_ref.1) | copy-start | bytes 2359300
  2.8 0.9 copy-start.1
  3.7 0.8 copy-start.3
  4.5 0.8 copy-start.4
  5.4 0.7 copy-start.5

commit v3 on v2

--- a/solution.py
+++ b/solution.py
@@ -214,12 +214,12 @@
 
 def mlp_kernel(
     n,
-    emb_ref,
     proj_ref,
-    gain_ref,
-    bias_ref,
-    up_bias_ref,
-    cot_ref,
+    emb_hbm,
+    gain_hbm,
+    bias_hbm,
+    up_bias_hbm,
+    cot_hbm,
     up_hbm,
     down_hbm,
     out_ref,
@@ -230,6 +230,11 @@
     grad_emb_ref,
     grad_proj_ref,
     sums_ref,
+    emb_ref,
+    gain_ref,
+    bias_ref,
+    up_bias_ref,
+    cot_ref,
     pairs,
     compressed,
     folded,
@@ -245,8 +250,12 @@
     down_ref,
     std_in,
     std_rows,
+    gh_pair_send,
+    gh_pair_recv,
     gh_send,
     gh_recv,
+    pre_pair_send,
+    pre_pair_recv,
     pre_send,
     pre_recv,
     act_all,
@@ -258,10 +267,16 @@
     down_sem,
     std_ss,
     std_rs,
+    gh_pair_ss,
+    gh_pair_rs,
     gh_ss,
     gh_rs,
+    pre_pair_ss,
+    pre_pair_rs,
     pre_ss,
     pre_rs,
+    pass_ss,
+    small_sem,
     act_ss,
     act_rs,
     back_ss,
@@ -291,20 +306,50 @@
             down_hbm.at[pl.ds(start, width), :], down_ref.at[j], down_sem.at[j]
         )
 
-    def loop(step_fn):
+    half_n = n // 2
+    core = lax.rem(me, 2)
+    place = me // 2
+    sibling = me + 1 - 2 * core
+
+    def places(step_fn):
         def step(k, carry):
-            step_fn(lax.rem(me + k, n))
+            step_fn(lax.rem(place + k, half_n))
             return carry
 
-        lax.fori_loop(1, n + 1, step, 0)
-
-    loop(lambda j: down_copy(j).start())
-    loop(lambda j: up_copy(j).start())
+        lax.fori_loop(1, half_n + 1, step, 0)
+
+    def other_places(step_fn):
+        def step(k, carry):
+            step_fn(lax.rem(place + k, half_n))
+            return carry
+
+        lax.fori_loop(1, half_n, step, 0)
+
+    small = [
+        pltpu.make_async_copy(source, target, small_sem.at[i])
+        for i, (source, target) in enumerate(
+            (
+                (emb_hbm, emb_ref),
+                (cot_hbm, cot_ref),
+                (gain_hbm, gain_ref),
+                (bias_hbm.at[me], bias_ref),
+                (up_bias_hbm.at[me], up_bias_ref),
+            )
+        )
+    ]
+    for copy in small:
+        copy.start()
+    places(lambda p: down_copy(2 * p + 1 - core).start())
+    places(lambda p: down_copy(2 * p + core).start())
+    places(lambda p: up_copy(2 * p + 1 - core).start())
+    places(lambda p: up_copy(2 * p + core).start())
     await_peers = greet(n, me)
 
     def whole_sum(values):
         return jnp.sum(jnp.sum(values, axis=1, keepdims=True), axis=0, keepdims=True)
 
+    for copy in small:
+        copy.wait()
     inv_scales = []
     for b in range(own):
         sample = emb_ref[b]
@@ -332,63 +377,99 @@
     await_peers()
 
     std = Exchange(n, me, standard_ref, std_in, std_ss, std_rs)
-    gh = Exchange(n, me, gh_send, gh_recv, gh_ss, gh_rs)
-    pre = Exchange(n, me, pre_send, pre_recv, pre_ss, pre_rs)
-    act = Exchange(n, me, act_all.at[me], act_all, act_ss, act_rs, same=True)
+
+    def reduce_blocks(part_fn, pair_send, pair_recv, send, recv, pair_ss, pair_rs, ss, rs):
+        def to_sibling(p):
+            return remote(
+                pair_send.at[p], pair_recv.at[p], pair_ss.at[p], pair_rs.at[p], sibling
+            )
+
+        def to_owner(p):
+            return remote(send.at[p], recv.at[place], ss.at[p], rs.at[place], 2 * p + core)
+
+        def from_place(p):
+            return remote(send.at[p], recv.at[p], ss.at[p], rs.at[p], 2 * p + core)
+
+        def first(p):
+            pair_send[p] = part_fn(2 * p + 1 - core).astype(jnp.bfloat16)
+            to_sibling(p).start()
+
+        def second(p):
+            part = part_fn(2 * p + core)
+            to_sibling(p).wait_recv()
+            part = (part + pair_recv[p].astype(jnp.float32)).astype(jnp.bfloat16)
+
+            @pl.when(p != place)
+            def _():
+                send[p] = part
+                to_owner(p).start()
+
+            @pl.when(p == place)
+            def _():
+                recv[place] = part
+
+        places(first)
+        places(second)
+
+        def result():
+            other_places(lambda p: from_place(p).wait_recv())
+            total = recv[0].astype(jnp.float32)
+            for p in range(1, half_n):
+                total = total + recv[p].astype(jnp.float32)
+            return total
+
+        def finish():
+            places(lambda p: to_sibling(p).wait_send())
+            other_places(lambda p: to_owner(p).wait_send())
+
+        return result, finish
+
     back = Exchange(n, me, back_send, back_ref, back_ss, back_rs)
     sums = Exchange(n, me, sums_own, sums_ref, sums_ss, sums_rs, same=True)
 
     std.send_all()
     std_in[me] = standard_ref[me]
 
-    def hidden_step(j):
+    def hidden_part(j):
         down_copy(j).wait()
-        part = lax.dot_general(
+        return lax.dot_general(
             cot_ref[...], down_ref[j], (((1,), (1,)), ((), ())), preferred_element_type=jnp.float32
-        ).astype(jnp.bfloat16)
-
-        @pl.when(j != me)
-        def _():
-            gh_send[j] = part
-            gh.send(j)
-
-        @pl.when(j == me)
-        def _():
-            gh_recv[me] = part
-
-    loop(hidden_step)
+        )
+
+    gh_result, gh_finish = reduce_blocks(
+        hidden_part,
+        gh_pair_send,
+        gh_pair_recv,
+        gh_send,
+        gh_recv,
+        gh_pair_ss,
+        gh_pair_rs,
+        gh_ss,
+        gh_rs,
+    )
 
     std.receive_all()
     for j in range(n):
         std_rows[own * j : own * (j + 1), :] = std_in[j].astype(jnp.float32)
-    columns_ref[...] = (std_rows[...] * gain_ref[me] + bias_ref[me]).astype(jnp.bfloat16)
-
-    def preact_step(j):
+    columns_ref[...] = (std_rows[...] * gain_ref[me] + bias_ref[...]).astype(jnp.bfloat16)
+
+    def preact_part(j):
         up_copy(j).wait()
-        part = jnp.dot(
-            columns_ref[...], up_ref[j], preferred_element_type=jnp.float32
-        ).astype(jnp.bfloat16)
-
-        @pl.when(j != me)
-        def _():
-            pre_send[j] = part
-            pre.send(j)
-
-        @pl.when(j == me)
-        def _():
-            pre_recv[me] = part
-
-    loop(preact_step)
-
-    gh.receive_all()
-    grad_hidden = gh_recv[0].astype(jnp.float32)
-    for j in range(1, n):
-        grad_hidden = grad_hidden + gh_recv[j].astype(jnp.float32)
-    pre.receive_all()
-    preact = pre_recv[0].astype(jnp.float32)
-    for j in range(1, n):
-        preact = preact + pre_recv[j].astype(jnp.float32)
-    preact = preact + up_bias_ref[me]
+        return jnp.dot(columns_ref[...], up_ref[j], preferred_element_type=jnp.float32)
+
+    pre_result, pre_finish = reduce_blocks(
+        preact_part,
+        pre_pair_send,
+        pre_pair_recv,
+        pre_send,
+        pre_recv,
+        pre_pair_ss,
+        pre_pair_rs,
+        pre_ss,
+        pre_rs,
+    )
+    grad_hidden = gh_result()
+    preact = pre_result() + up_bias_ref[...]
     root = math.sqrt(2 / math.pi)
     square = preact * preact
     bent = jnp.tanh(root * preact * (1.0 + 0.044715 * square))
@@ -396,7 +477,12 @@
     slope = half + 0.5 * preact * (1.0 - bent * bent) * (root * (1.0 + 3 * 0.044715 * square))
     act_all[me, 0] = (preact * half).astype(jnp.bfloat16)
     act_all[me, 1] = (grad_hidden * slope).astype(jnp.bfloat16)
-    act.send_all()
+
+    def act_copy(j, peer, sent):
+        return remote(act_all.at[j], act_all.at[j], sent, act_rs.at[j], peer)
+
+    act_copy(me, sibling, act_ss.at[sibling]).start()
+    other_places(lambda p: act_copy(me, 2 * p + core, act_ss.at[2 * p + core]).start())
 
     def gather_step(j):
         columns = pl.ds(pl.multiple_of(j * width, width), width)
@@ -414,13 +500,21 @@
     back_acc[...] = jnp.zeros_like(back_acc)
     gather_step(me)
 
+    act_copy(sibling, sibling, act_ss.at[sibling]).wait_recv()
+    gather_step(sibling)
+
     def arrive_step(k, carry):
-        j = lax.rem(me + n - k, n)
-        act.receive(j)
-        gather_step(j)
+        p = lax.rem(place + half_n - k, half_n)
+        near = 2 * p + core
+        far = 2 * p + 1 - core
+        act_copy(near, sibling, act_ss.at[near]).wait_recv()
+        act_copy(near, sibling, pass_ss.at[near]).start()
+        gather_step(near)
+        act_copy(far, sibling, act_ss.at[far]).wait_recv()
+        gather_step(far)
         return carry
 
-    lax.fori_loop(1, n, arrive_step, 0)
+    lax.fori_loop(1, half_n, arrive_step, 0)
 
     grad_normed = back_acc[...].astype(jnp.bfloat16)
     wide = grad_normed.astype(jnp.float32)
@@ -434,8 +528,12 @@
     sums.send_all()
     sums_ref[me] = sums_own[...]
     out_ref[...] = out_acc[...].astype(jnp.bfloat16)
-    for exchange in (std, gh, pre, act):
-        exchange.finish()
+    std.finish()
+    gh_finish()
+    pre_finish()
+    act_copy(me, sibling, act_ss.at[sibling]).wait_send()
+    other_places(lambda p: act_copy(me, 2 * p + core, act_ss.at[2 * p + core]).wait_send())
+    other_places(lambda p: act_copy(2 * p + core, sibling, pass_ss.at[2 * p + core]).wait_send())
     part = Exchange(n, me, part_send, part_recv, part_ss, part_rs)
     total = Exchange(n, me, own_total, grad_proj_ref, total_ss, total_rs, same=True)
     back.receive_all()
@@ -512,9 +610,14 @@
             shape((n, samples // n, kept), f32),
             shape((n, 2, features), f32),
         ),
-        in_specs=[vmem] * 6 + [hbm] * 2,
+        in_specs=[vmem] + [hbm] * 7,
         out_specs=[vmem] * 8,
         scratch_shapes=[
+            pltpu.VMEM(embeddings.shape, bf16),
+            pltpu.VMEM((n, 1, features), f32),
+            pltpu.VMEM((1, features), f32),
+            pltpu.VMEM((1, width), f32),
+            pltpu.VMEM((rows, features), bf16),
             pltpu.VMEM((own, samples, samples), bf16),
             pltpu.VMEM((own, samples, kept), bf16),
             pltpu.VMEM((own, depth, kept), f32),
@@ -530,17 +633,16 @@
             pltpu.VMEM((n, width, features), bf16),
             pltpu.VMEM((n, own, features), bf16),
             pltpu.VMEM((rows, features), f32),
-            pltpu.VMEM((n, rows, width), bf16),
-            pltpu.VMEM((n, rows, width), bf16),
-            pltpu.VMEM((n, rows, width), bf16),
-            pltpu.VMEM((n, rows, width), bf16),
+        ]
+        + [pltpu.VMEM((n // 2, rows, width), bf16)] * 8
+        + [
             pltpu.VMEM((n, 2, rows, width), bf16),
             pltpu.VMEM((n, own, features), bf16),
             pltpu.VMEM((2, features), f32),
             pltpu.VMEM((rows, features), f32),
             pltpu.VMEM((rows, features), f32),
         ]
-        + [pltpu.SemaphoreType.DMA((n,))] * 18,
+        + [pltpu.SemaphoreType.DMA((n,))] * 24,
         compiler_params=pltpu.CompilerParams(
             collective_id=0, has_side_effects=True, vmem_limit_bytes=48 * 2**20
         ),
@@ -551,8 +653,8 @@
         ),
         name="perceptron",
     )(
+        projection,
         embeddings,
-        projection,
         norm_gain.reshape(n, 1, features),
         norm_bias.reshape(n, 1, features),
         up_bias.reshape(n, 1, width),
@@ -562,17 +664,35 @@
     )
 
 
-def weight_kernel(columns_ref, grad_preact_ref, hidden_ref, cot_ref, up_ref, down_ref):
+def weight_kernel(
+    columns_ref,
+    grad_preact_ref,
+    hidden_ref,
+    cot_ref,
+    out_in,
+    emb_in,
+    sums_in,
+    up_ref,
+    down_ref,
+    out_ref,
+    emb_ref,
+    gain_ref,
+    bias_ref,
+):
     up_ref[...] = contract_rows(columns_ref[...], grad_preact_ref[...])
     down_ref[...] = contract_rows(hidden_ref[...], cot_ref[...])
-
-
-def weight_grads(columns, grad_preact, hidden, cotangent):
+    out_ref[...] = out_in[...]
+    emb_ref[...] = emb_in[...]
+    gain_ref[...] = sums_in[:, 0:1, :]
+    bias_ref[...] = sums_in[:, 1:2, :]
+
+
+def finish_grads(columns, grad_preact, hidden, cotangent, out, grad_embeddings, sums):
     rows, features = columns.shape
     units = hidden.shape[1]
-    steps = math.gcd(features, units) // 128
-    while steps > 16:
-        steps //= 2
+    own, samples, depth = grad_embeddings.shape
+    n = sums.shape[0]
+    steps = math.gcd(math.gcd(features, units) // 128, math.gcd(n, samples // 16))
 
     def part(extent):
         return pl.BlockSpec((rows, extent // steps), lambda i: (0, i))
@@ -583,37 +703,63 @@
     def result(height, width):
         return pl.BlockSpec((height // steps, width), lambda i: (i, 0))
 
+    def lead(second):
+        return pl.BlockSpec((n // steps, second, features), lambda i: (i, 0, 0))
+
+    emb = pl.BlockSpec((own, samples // steps, depth), lambda i: (0, i, 0))
+    shape = jax.ShapeDtypeStruct
     return pl.pallas_call(
         weight_kernel,
         grid=(steps,),
         out_shape=(
-            jax.ShapeDtypeStruct((features, units), jnp.float32),
-            jax.ShapeDtypeStruct((units, features), jnp.float32),
+            shape((features, units), jnp.float32),
+            shape((units, features), jnp.float32),
+            shape(out.shape, out.dtype),
+            shape(grad_embeddings.shape, grad_embeddings.dtype),
+            shape((n, 1, features), jnp.float32),
+            shape((n, 1, features), jnp.float32),
         ),
-        in_specs=[part(features), whole(units), part(units), whole(features)],
-        out_specs=(result(features, units), result(units, features)),
+        in_specs=[
+            part(features),
+            whole(units),
+            part(units),
+            whole(features),
+            part(features),
+            emb,
+            lead(2),
+        ],
+        out_specs=(
+            result(features, units),
+            result(units, features),
+            part(features),
+            emb,
+            lead(1),
+            lead(1),
+        ),
         compiler_params=pltpu.CompilerParams(vmem_limit_bytes=40 * 2**20),
         name="weight_grads",
-    )(columns, grad_preact, hidden, cotangent)
+    )(columns, grad_preact, hidden, cotangent, out, grad_embeddings, sums)
 
 
 def body(embeddings, projection, norm_gain, norm_bias, up_weight, up_bias, down_weight, cotangent):
     n = lax.axis_size("dp")
     own_rows = embeddings.shape[0]
-    if (up_weight.shape[1] // n) % 128 or cotangent.shape[0] % 16:
+    if n % 2 or (up_weight.shape[1] // n) % 128 or cotangent.shape[0] % 16:
         return plain_body(
             embeddings, projection, norm_gain, norm_bias, up_weight, up_bias, down_weight, cotangent
         )
     out, columns, hidden, grad_preact, grad_up_bias, grad_embeddings, grad_projection, sums = mlp(
         embeddings, projection, norm_gain, norm_bias, up_weight, up_bias, down_weight, cotangent
     )
-    grad_up, grad_down = weight_grads(columns, grad_preact, hidden, cotangent)
+    grad_up, grad_down, out, grad_embeddings, grad_gain, grad_bias = finish_grads(
+        columns, grad_preact, hidden, cotangent, out, grad_embeddings, sums
+    )
     return (
         out,
         grad_embeddings,
         grad_projection.reshape(projection.shape),
-        sums[:, 0, :].reshape(-1),
-        sums[:, 1, :].reshape(-1),
+        grad_gain.reshape(-1),
+        grad_bias.reshape(-1),
         grad_up,
         grad_up_bias.reshape(-1),
         grad_down,

time: 95.1 us -> 82.2 us (0.86)
  Pallas kernels: 85 us -> 74.3 us
  local copies, waits for them, and re-layouts: 9.06 us -> 6.79 us
    pallas_call x1, Pallas kernels: 73.6 us -> 62.6 us  [mlp(): pl.pallas_call(functools.partial(mlp_kernel, n), out_shape=(shape((rows,...]
    unnamed x17 -> x15, local copies, waits for them, and re-layouts: 8.31 us -> 6.79 us
where the time goes in v3:
time: 82.2 us; the launch traced here: 81.8 us
  Pallas kernels  74.3 us (90%)
  local copies, waits for them, and re-layouts  6.79 us (8%)
    pallas_call x1, Pallas kernels, mlp(): pl.pallas_call(functools.partial(mlp_kernel, n), out_shape=(shape((rows,...  62.6 us
    pallas_call x1, Pallas kernels, finish_grads(): pl.pallas_call(weight_kernel, grid=(steps,), out_shape=(shape((features,...  11.8 us
    unnamed x15, local copies, waits for them, and re-layouts  6.79 us

profile of v3, /device:TPU:0, one launch (start us, length us, event | category | flops | bytes accessed | tf_op | source)
XLA Modules:
  0.0 81.8 jit_solution(14049897161478524542)
XLA Ops:
  0.6 0.0 copy-start.2
  0.6 1.0 %copy.16.proj_ref = bf16[512,64]{1,0:T(8,128)(2,1)S(1)} copy(bf16[512,64]{0,1:T(8,128)(2,1)} %param.9) | data formatting | bytes 131072 | tf_op args[1]
  1.6 0.0 copy-start
  1.7 1.1 %copy-done = bf16[3,512,256]{2,1,0:T(8,128)(2,1)S(1)} copy-done((bf16[3,512,256]{2,1,0:T(8,128)(2,1)S(1)}, bf16[3,512,256]{2,1,0:T(8,128)(2,1)}, u32[]{:S(2)}) %copy-start) | copy-done | bytes 786456
  2.8 0.0 copy-start.1
  2.8 0.9 %copy-done.1 = bf16[48,1024]{1,0:T(8,128)(2,1)S(1)} copy-done((bf16[48,1024]{1,0:T(8,128)(2,1)S(1)}, bf16[48,1024]{1,0:T(8,128)(2,1)}, u32[]{:S(2)}) %copy-start.1) | copy-done | bytes 98328
  3.7 0.0 copy-start.3
  3.7 0.8 %copy-done.3 = f32[16384]{0:T(1024)S(1)} copy-done((f32[16384]{0:T(1024)S(1)}, f32[16384]{0:T(1024)}, u32[]{:S(2)}) %copy-start.3) | copy-done | bytes 65560
  4.5 0.0 copy-start.4
  4.5 0.8 %copy-done.4 = f32[16384]{0:T(1024)S(1)} copy-done((f32[16384]{0:T(1024)S(1)}, f32[16384]{0:T(1024)}, u32[]{:S(2)}) %copy-start.4) | copy-done | bytes 65560
  5.4 0.0 copy-start.5
  5.4 0.7 copy-done.5
  6.1 62.6 %perceptron.1 = (bf16[48,1024]{1,0:T(8,128)(2,1)S(1)}, bf16[48,1024]{1,0:T(8,128)(2,1)S(1)}, bf16[48,4096]{1,0:T(8,128)(2,1)S(1)}, bf16[48,4096]{1,0:T(8,128)(2,...) custom-call(bf16[512,64]{1,0:T(8,128)(2,1)S(1)} %copy.16.proj_ref, ...), custom_call_target="tpu_custom_call" | custom-call | flops 1610612736 | bytes 16777216 | tf_op jit(solution)/shard_map/perceptron/pallas_call | solution.py:601
  68.7 0.8 copy.17
  69.4 0.0 copy-done.2
  69.4 11.8 %weight_grads.1 = (f32[1024,4096]{1,0:T(8,128)}, f32[4096,1024]{1,0:T(8,128)}, bf16[48,1024]{1,0:T(8,128)(2,1)}, bf16[3,512,256]{2,1,0:T(8,128)(2,1)}, f32[16,1,1024]{2,1,0:T(1,128)}, /*index=5*/f32[16,1,1024]{2,1,0:T(1,128)}) custom-call(bf16[48,1024]{1,0:T(8,128)(2,1)S(1)} %get-tuple-element.22.columns_ref, ...), custom_call_target="tpu_custom_call" | custom-call | tf_op jit(solution)/shard_map/weight_grads/pallas_call | solution.py:711
  81.2 0.6 copy.19
Async XLA Ops:
  0.6 68.8 %copy-start.2 = (bf16[48,1024]{1,0:T(8,128)(2,1)S(1)}, bf16[48,1024]{1,0:T(8,128)(2,1)}, u32[]{:S(2)}) copy-start(bf16[48,1024]{1,0:T(8,128)(2,1)} %cot_ref.1) | copy-start | bytes 294916
  1.6 1.1 %copy-start = (bf16[3,512,256]{2,1,0:T(8,128)(2,1)S(1)}, bf16[3,512,256]{2,1,0:T(8,128)(2,1)}, u32[]{:S(2)}) copy-start(bf16[3,512,256]{2,1,0:T(8,128)(2,1)} %emb_hbm.1) | copy-start | bytes 2359300
  2.8 0.9 %copy-start.1 = (bf16[48,1024]{1,0:T(8,128)(2,1)S(1)}, bf16[48,1024]{1,0:T(8,128)(2,1)}, u32[]{:S(2)}) copy-start(bf16[48,1024]{1,0:T(8,128)(2,1)} %cot_ref.1) | copy-start | bytes 294916
  3.7 0.8 %copy-start.3 = (f32[16384]{0:T(1024)S(1)}, f32[16384]{0:T(1024)}, u32[]{:S(2)}) copy-start(f32[16384]{0:T(1024)} %param.10) | copy-start | bytes 196612
  4.5 0.8 %copy-start.4 = (f32[16384]{0:T(1024)S(1)}, f32[16384]{0:T(1024)}, u32[]{:S(2)}) copy-start(f32[16384]{0:T(1024)} %param.11) | copy-start | bytes 196612
  5.4 0.7 copy-start.5
